TPU v7x, 128 devices: a whole 4x4x4 slice. The times are simulated.
128 devices in a mesh: section: 4 (over x_hi, core), replica: 4 (over z), tensor: 8 (over y, x_lo).
Axes of the slice: x: 4 (x_hi: 2, x_lo: 2; x = x_hi * 2 + x_lo), y: 4, z: 4, core: 2. Of those that a mesh axis runs over, the one named last changes fastest.
Arguments:
- out_grad: bfloat16 [4, 8, 128, 1024], P('replica', None, 'tensor'), may hold values from -6 to 6
- relu_mask: int32 [4, 4, 8, 128, 4096], P('section', 'replica', None, None, 'tensor'), may hold values from 0 to 255
- w_in: bfloat16 [4, 1024, 32768], P('section', None, 'tensor'), may hold values from -0.1875 to 0.1875
- w_out: bfloat16 [4, 32768, 1024], P('section', 'tensor'), may hold values from -0.03125 to 0.03125
- route: int32 [3, 8, 4], replicated, may hold values from 0 to 3, each once within a row
Outputs:
- in_grads: bfloat16 [4, 4, 8, 128, 1024], P('section', 'replica', None, 'tensor')
Inputs may be any that keep to these rules, and one draw needn't show every extreme that they name: Each route[s, m, :] is a permutation of the replicas.
All inputs are finite; a program needn't handle non-finite values.
Results may differ from a plain program's by a relative error of at most 0.0095.
Values may be sent and summed in bfloat16 or wider, within the bound.
No kernel may reach another device: no remote copies, remote signals or barrier semaphores. Data moves between devices by JAX's collectives and lax.ppermute only.
A program may use at most 128 MiB of HBM per device.

v0:
```python
import functools

import jax
import jax.numpy as jnp
from jax import lax
from jax.experimental import pallas as pl
from jax.experimental.pallas import tpu as pltpu
from jax.sharding import PartitionSpec as P

N_CHUNK = 2
BLOCK = 1024
COLUMNS = 512
GROUP = BLOCK // 8
MIB = 1024 * 1024
LAST_DIMS = (((1,), (1,)), ((), ()))
SCALARS = pl.BlockSpec(memory_space=pltpu.SMEM)
WHOLE = pl.BlockSpec(memory_space=pltpu.VMEM)
OUTSIDE = pl.BlockSpec(memory_space=pltpu.HBM)


def turn(section, slot, n_section):
    offset = slot - (n_section - 1 - section)
    return jnp.clip(offset, 0, N_CHUNK - 1), (offset >= 0) & (offset < N_CHUNK)


def expand_kernel(chunk, facts_ref, words_ref, out_ref, held_ref, ones_ref, spread_ref, sems):
    sources = words_ref.shape[0]
    micro = held_ref.shape[0]
    parts, rows = out_ref.shape[:2]
    tokens = rows // micro

    def read(m):
        at = chunk * micro + m
        source = 0 if sources == 1 else facts_ref[1 + at]
        return pltpu.make_async_copy(words_ref.at[source, at], held_ref.at[m], sems.at[0, m])

    def write(m):
        place = pl.ds(pl.multiple_of(m * tokens, tokens), tokens)
        return pltpu.make_async_copy(ones_ref.at[m], out_ref.at[:, place], sems.at[1, m])

    for m in range(micro):
        read(m).start()
    word = lax.broadcasted_iota(jnp.int32, spread_ref.shape, 0)
    unit = lax.broadcasted_iota(jnp.int32, spread_ref.shape, 1)
    spread_ref[...] = jnp.where(
        jnp.right_shift(unit, 3) == word, jnp.float32(1), jnp.float32(0)
    ).astype(jnp.bfloat16)
    lane = lax.broadcasted_iota(jnp.int32, (1, BLOCK), 1)
    bit = jnp.left_shift(jnp.int32(1), jnp.bitwise_and(lane, 7))

    @pl.loop(0, micro)
    def _(m):
        read(m).wait()
        for at in range(held_ref.shape[2] // GROUP):
            words = held_ref[m, :, at * GROUP : (at + 1) * GROUP]
            value = jnp.dot(words, spread_ref[...], preferred_element_type=jnp.float32)
            on = jnp.bitwise_and(value.astype(jnp.int32), bit) != 0
            ones = jnp.where(on, jnp.float32(1), jnp.float32(0)).astype(jnp.bfloat16)
            ones_ref[m, :, :, at * BLOCK : (at + 1) * BLOCK] = ones.reshape(parts, tokens, BLOCK)
        write(m).start()

    for m in range(micro):
        write(m).wait()


def expand(chunk, parts, facts, words):
    _, micro, tokens, count = words.shape
    micro //= N_CHUNK
    shape = (parts, micro * tokens // parts, 8 * count)
    return pl.pallas_call(
        functools.partial(expand_kernel, chunk),
        in_specs=[SCALARS, OUTSIDE],
        out_specs=OUTSIDE,
        out_shape=jax.ShapeDtypeStruct(shape, jnp.bfloat16),
        scratch_shapes=[
            pltpu.VMEM((micro, tokens, count), jnp.bfloat16),
            pltpu.VMEM((micro, parts, tokens // parts, 8 * count), jnp.bfloat16),
            pltpu.VMEM((GROUP, BLOCK), jnp.bfloat16),
            pltpu.SemaphoreType.DMA((2, micro)),
        ],
        compiler_params=pltpu.CompilerParams(vmem_limit_bytes=56 * MIB),
        cost_estimate=pl.CostEstimate(
            flops=micro * tokens * count * 8 * 512,
            bytes_accessed=micro * tokens * count * 18,
            transcendentals=0,
        ),
    )(facts, words)


def block_kernel(holders, facts_ref, x_ref, w_out_ref, w_in_ref, *refs):
    mask_refs, refs = refs[: len(holders)], refs[len(holders) :]
    out_ref, w_out_buf, w_in_buf, mask_buf, hidden_ref, sems = refs
    parts, rows, width = x_ref.shape
    total = parts * rows
    n_up, n_down = w_out_ref.shape[0] // BLOCK, width // COLUMNS

    def place(at, size):
        return pl.ds(at * size if isinstance(at, int) else pl.multiple_of(at * size, size), size)

    def up(at):
        units = place(at, BLOCK)
        return pltpu.make_async_copy(w_out_ref.at[units], w_out_buf.at[units], sems.at[0, at])

    def mask(at, ref):
        units = place(at, BLOCK)
        return pltpu.make_async_copy(ref.at[:, :, units], mask_buf.at[:, :, units], sems.at[1, at])

    def down(at):
        columns = place(at, COLUMNS)
        return pltpu.make_async_copy(w_in_ref.at[columns], w_in_buf.at[columns], sems.at[2, at])

    for at in range(n_up):
        up(at).start()
        if len(holders) == 1:
            mask(at, mask_refs[0]).start()
        else:
            for holder, ref in zip(holders, mask_refs):

                @pl.when(facts_ref[0] == holder)
                def _(at=at, ref=ref):
                    mask(at, ref).start()

    for at in range(n_down):
        down(at).start()

    @pl.loop(0, n_up)
    def _(at):
        up(at).wait()
        mask(at, mask_refs[0]).wait()
        units = place(at, BLOCK)
        pre = lax.dot_general(
            x_ref[...].reshape(total, width),
            w_out_buf[units, :],
            LAST_DIMS,
            preferred_element_type=jnp.float32,
        )
        hidden_ref[:, units] = pre.astype(jnp.bfloat16) * mask_buf[:, :, units].reshape(total, BLOCK)

    @pl.loop(0, n_down)
    def _(at):
        down(at).wait()
        columns = place(at, COLUMNS)
        term = lax.dot_general(
            hidden_ref[...], w_in_buf[columns, :], LAST_DIMS, preferred_element_type=jnp.float32
        )
        out_ref[:, :, columns] = term.astype(jnp.bfloat16).reshape(parts, rows, COLUMNS)


def block_sums(facts, x, w_out, w_in, masks):
    parts, rows, width = x.shape
    total = parts * rows
    units = w_out.shape[0]
    return pl.pallas_call(
        functools.partial(block_kernel, tuple(masks)),
        in_specs=[SCALARS, WHOLE] + [OUTSIDE] * (2 + len(masks)),
        out_specs=WHOLE,
        out_shape=jax.ShapeDtypeStruct((parts, rows, width), jnp.bfloat16),
        scratch_shapes=[
            pltpu.VMEM((units, width), jnp.bfloat16),
            pltpu.VMEM((width, units), jnp.bfloat16),
            pltpu.VMEM((parts, rows, units), jnp.bfloat16),
            pltpu.VMEM((total, units), jnp.bfloat16),
            pltpu.SemaphoreType.DMA((3, max(units // BLOCK, width // COLUMNS))),
        ],
        compiler_params=pltpu.CompilerParams(vmem_limit_bytes=52 * MIB),
        cost_estimate=pl.CostEstimate(
            flops=4 * total * width * units, bytes_accessed=4 * width * units, transcendentals=0
        ),
    )(facts, x, w_out, w_in, *masks.values())


def address_kernel(n_section, facts_ref, *refs):
    *grads_refs, out_ref = refs
    n_replica, micro, tokens, _ = out_ref.shape
    per_chunk = micro // N_CHUNK
    for chunk in range(N_CHUNK):
        for section in range(n_section):

            @pl.when(facts_ref[0] == section)
            def _(chunk=chunk, section=section):
                value = grads_refs[chunk + n_section - 1 - section]
                for i in range(per_chunk):
                    m = chunk * per_chunk + i
                    rows = value[i * tokens : (i + 1) * tokens, :]
                    for q in range(n_replica):
                        mine = jnp.where(facts_ref[1 + m] == q, rows, jnp.zeros_like(rows))
                        out_ref[q, m] = mine


def address(n_section, n_replica, micro, facts, grads):
    rows, width = grads[0].shape
    return pl.pallas_call(
        functools.partial(address_kernel, n_section),
        in_specs=[SCALARS] + [WHOLE] * len(grads),
        out_specs=WHOLE,
        out_shape=jax.ShapeDtypeStruct((n_replica, micro, rows * N_CHUNK // micro, width), jnp.bfloat16),
        compiler_params=pltpu.CompilerParams(vmem_limit_bytes=8 * MIB),
    )(facts, *grads)


def shards(out_grad, relu_mask, w_in, w_out, route):
    n_section = lax.axis_size("section")
    n_replica = lax.axis_size("replica")
    n_tensor = lax.axis_size("tensor")
    micro, tokens, width = out_grad.shape[1:]
    section = lax.axis_index("section")
    replica = lax.axis_index("replica")
    per_chunk = micro // N_CHUNK
    last = n_section - 1
    slots = N_CHUNK + last
    w_in_local, w_out_local = w_in[0], w_out[0]
    entry = out_grad[0].reshape(N_CHUNK, per_chunk * tokens, width)
    names = jnp.arange(n_replica, dtype=jnp.int32)

    def facts_of(route):
        belongs = jnp.broadcast_to(replica, (micro,)).astype(jnp.int32)
        for hop in range(last - 1, -1, -1):
            moved = jnp.sum(jnp.where(belongs[:, None] == names, route[hop], 0), axis=1)
            belongs = jnp.where(section <= hop, moved, belongs)
        return jnp.concatenate([section.astype(jnp.int32).reshape(1), belongs])

    def swap(value):
        return lax.all_to_all(value, "tensor", 0, 0)

    def work(facts, rows, masks):
        x = swap(jnp.broadcast_to(rows[None], (n_tensor,) + rows.shape))
        partial = block_sums(facts, x, w_out_local, w_in_local, masks)
        total = jnp.sum(swap(partial).astype(jnp.float32), axis=0)
        return (rows.astype(jnp.float32) + total).astype(jnp.bfloat16)

    def expand_all(facts, words):
        return [expand(at, n_tensor, facts, words) for at in range(N_CHUNK)]

    def start(entry, relu_mask, route):
        facts = jnp.where(jnp.arange(1 + micro) == 0, section, replica).astype(jnp.int32)
        masks = expand_all(facts, relu_mask[0].astype(jnp.bfloat16))
        return [work(facts, entry[0], {last: masks[0]}), facts] + masks

    def rest(entry, relu_mask, route):
        words = relu_mask[0, 0].astype(jnp.bfloat16)
        copies = jnp.broadcast_to(words[None], (n_replica,) + words.shape)
        facts = facts_of(route)
        return [entry[0], facts] + expand_all(facts, lax.all_to_all(copies, "replica", 0, 0))

    grads = []
    for slot in range(slots):
        active = turn(section, slot, n_section)[1]
        holders = {}
        for holder in range(last + 1):
            chunk = slot - (last - holder)
            if 0 <= chunk < N_CHUNK:
                holders[holder] = chunk
        if slot == 0:
            result, facts, *masks = lax.cond(active, start, rest, entry, relu_mask, route)
        else:
            rows = carried
            if last in holders:
                rows = jnp.where(section == last, entry[holders[last]], rows)
            result = lax.cond(
                active,
                lambda rows, *masks: work(
                    facts, rows, {holder: masks[chunk] for holder, chunk in holders.items()}
                ),
                lambda rows, *masks: rows,
                rows,
                *masks,
            )
        grads.append(result)
        if slot < slots - 1:
            carried = lax.ppermute(result, "section", [(s, s - 1) for s in holders if s > 0])
    outgoing = address(n_section, n_replica, micro, facts, grads)
    got = lax.all_to_all(outgoing, "replica", 0, 0)
    done = jnp.sum(got.astype(jnp.float32), axis=0).astype(jnp.bfloat16)
    return done[None, None]


def solution(mesh):
    in_specs = (
        P("replica", None, "tensor", None),
        P("section", "replica", None, None, "tensor"),
        P("section", None, "tensor"),
        P("section", "tensor", None),
        P(),
    )
    out_specs = P("section", "replica", None, "tensor", None)
    return jax.shard_map(shards, mesh=mesh, in_specs=in_specs, out_specs=out_specs, check_vma=False)
```

profile of v0, /device:TPU:0, one launch (start us, length us, event | category | flops | bytes accessed | tf_op | source)
XLA Modules:
  0.0 262.3 jit_solution(16398689828095221736)
XLA Ops:
  0.0 69.4 %conditional.5 = (bf16[64,1024]{1,0:T(8,128)(2,1)S(1)}, s32[9]{0:T(128)}, bf16[8,64,4096]{2,1,0:T(8,128)(2,1)}, bf16[8,64,4096]{2,1,0:T(8,128)(2,1)}) conditional(s32[]{:T(128)} %convert_element_type.77, (bf16[2,64,1024]{2,1,0:T(8,128)(2,1)}, s32[]{:T(128)}, s32[]{:T(128)}, s32[4]{0:T(128)S(1)}, s32[3,8,4]{1,2,0:T(4,128)}, /*index=5*/s32[4]{0:T(128)S(1)}, ...), branch_computations={%region_0.4_spmd, %region_4.6_spmd} | conditional | flops 10739122176 | bytes 52560096 | solution.py:254
  0.0 1.9 convert_bitcast_fusion
  1.9 2.5 broadcast_in_dim.37
  4.3 5.5 %all-to-all-start = ((bf16[4,8,128,512]{3,2,1,0:T(8,128)(2,1)}), bf16[4,8,128,512]{3,2,1,0:T(8,128)(2,1)}, u32[]{:S(2)}, u32[]{:S(2)}) async-start(bf16[4,8,128,512]{3,2,1,0:T(8,128)(2,1)} %broadcast_in_dim.37), calls=%async_computation | async-start | bytes 8388608 | tf_op jit(solution)/shard_map/cond/branch_0_fun/all_to_all | solution.py:243
  10.1 0.1 fusion
  10.2 0.7 pad_add_fusion.facts_ref
  10.8 48.5 %all-to-all-done.words_ref = bf16[4,8,128,512]{3,2,1,0:T(8,128)(2,1)} async-done(((bf16[4,8,128,512]{3,2,1,0:T(8,128)(2,1)}), bf16[4,8,128,512]{3,2,1,0:T(8,128)(2,1)}, u32[]{:S(2)}, u32[]{:S(2)}) %all-to-all-start) | async-done | bytes 4194336 | tf_op jit(solution)/shard_map/cond/branch_0_fun/all_to_all | solution.py:243
  59.3 5.0 %branch_0_fun.2 = bf16[8,64,4096]{2,1,0:T(8,128)(2,1)} custom-call(s32[9]{0:T(128)} %pad_add_fusion.facts_ref, bf16[4,8,128,512]{3,2,1,0:T(8,128)(2,1)} %all-to-all-done.words_ref), custom_call_target="tpu_custom_call" | custom-call | flops 1073741824 | bytes 4718592 | tf_op jit(solution)/shard_map/cond/branch_0_fun/pallas_call | solution.py:70
  64.4 5.0 %branch_0_fun.3 = bf16[8,64,4096]{2,1,0:T(8,128)(2,1)} custom-call(s32[9]{0:T(128)} %pad_add_fusion.facts_ref, bf16[4,8,128,512]{3,2,1,0:T(8,128)(2,1)} %all-to-all-done.words_ref), custom_call_target="tpu_custom_call" | custom-call | flops 1073741824 | bytes 4718592 | tf_op jit(solution)/shard_map/cond/branch_0_fun/pallas_call | solution.py:70
  69.4 0.7 collective-permute-start
  70.1 0.9 slice.19
  71.1 0.7 collective-permute-start.1
  71.8 0.2 conditional.7
  72.0 1.3 collective-permute-start.2
  73.3 80.3 %collective-permute-done.2 = bf16[64,1024]{1,0:T(8,128)(2,1)S(1)} collective-permute-done((bf16[64,1024]{1,0:T(8,128)(2,1)S(1)}, bf16[64,1024]{1,0:T(8,128)(2,1)S(1)}, u32[]{:S(2)}, u32[]{:S(2)}) %collective-permute-start.2) | collective-permute-done | bytes 131104 | tf_op jit(solution)/shard_map/ppermute | solution.py:270
  153.6 47.3 %conditional.8 = (bf16[64,1024]{1,0:T(8,128)(2,1)S(1)}) conditional(s32[]{:T(128)} %convert_element_type.80, bf16[64,1024]{1,0:T(8,128)(2,1)S(1)} %collective-permute-done.2, (bf16[64,1024]{1,0:T(8,128)(2,1)S(1)}, s32[9]{0:T(128)}, bf16[4096,1024]{1,0:T(8,128)(2,1)}, bf16[1024,4096]{1,0:T(8,128)(2,1)}, bf16[8,64,4096]{2,1,0:T(8,128)(2,1)}, ...), branch_computations={%region_12.13_spmd, %region_13.15_spmd} | conditional | flops 8591114240 | bytes 23986184 | solution.py:259
  153.6 0.1 broadcast_in_dim.51
  153.7 16.1 %all_to_all.53.x_ref = bf16[8,64,1024]{2,1,0:T(8,128)(2,1)} all-to-all(bf16[8,64,1024]{2,1,0:T(8,128)(2,1)S(1)} %broadcast_in_dim.51), channel_id=1, replica_groups=mesh['section'=4,'replica'=4,'tensor'=8] {'tensor'}, dimensions={0} | all-to-all | bytes 2097152 | tf_op jit(solution)/shard_map/cond/branch_1_fun/all_to_all | solution.py:223
  169.8 13.1 %branch_1_fun.12 = bf16[8,64,1024]{2,1,0:T(8,128)(2,1)S(1)} custom-call(s32[9]{0:T(128)} %get-tuple-element.120.facts_ref, bf16[8,64,1024]{2,1,0:T(8,128)(2,1)} %all_to_all.53.x_ref, bf16[4096,1024]{1,0:T(8,128)(2,1)} %get-tuple-element.121.w_out_ref, bf16[1024,4096]{1,0:T(8,128)(2,1)} %get-tuple-element.122.w_in_ref, ...), custom_call_target="tpu_custom_call" | custom-call | flops 8589934592 | bytes 16777216 | tf_op jit(solution)/shard_map/cond/branch_1_fun/pallas_call | solution.py:153
  182.9 17.8 %all_to_all.54 = bf16[8,64,1024]{2,1,0:T(8,128)(2,1)S(1)} all-to-all(bf16[8,64,1024]{2,1,0:T(8,128)(2,1)S(1)} %branch_1_fun.12), channel_id=1, replica_groups=mesh['section'=4,'replica'=4,'tensor'=8] {'tensor'}, dimensions={0} | all-to-all | bytes 2097152 | tf_op jit(solution)/shard_map/cond/branch_1_fun/all_to_all | solution.py:223
  200.7 0.2 convert_reduce_fusion.3
  200.9 1.3 collective-permute-start.3
  202.2 3.0 %collective-permute-done.3 = bf16[64,1024]{1,0:T(8,128)(2,1)S(1)} collective-permute-done((bf16[64,1024]{1,0:T(8,128)(2,1)S(1)}, bf16[64,1024]{1,0:T(8,128)(2,1)S(1)}, u32[]{:S(2)}, u32[]{:S(2)}) %collective-permute-start.3) | collective-permute-done | bytes 131104 | tf_op jit(solution)/shard_map/ppermute | solution.py:270
  205.2 42.0 %conditional.9 = (bf16[64,1024]{1,0:T(8,128)(2,1)S(1)}) conditional(s32[]{:T(128)} %convert_element_type.81, bf16[64,1024]{1,0:T(8,128)(2,1)S(1)} %collective-permute-done.3, (bf16[64,1024]{1,0:T(8,128)(2,1)S(1)}, s32[9]{0:T(128)}, bf16[4096,1024]{1,0:T(8,128)(2,1)}, bf16[1024,4096]{1,0:T(8,128)(2,1)}, bf16[8,64,4096]{2,1,0:T(8,128)(2,1)}) %tuple.64), branch_computations={%region_15.16_spmd, %region_16.18_spmd} | conditional | flops 8591114240 | bytes 23986184 | solution.py:259
  205.2 0.1 broadcast_in_dim.52
  205.3 14.6 %all_to_all.55.x_ref = bf16[8,64,1024]{2,1,0:T(8,128)(2,1)} all-to-all(bf16[8,64,1024]{2,1,0:T(8,128)(2,1)S(1)} %broadcast_in_dim.52), channel_id=1, replica_groups=mesh['section'=4,'replica'=4,'tensor'=8] {'tensor'}, dimensions={0} | all-to-all | bytes 2097152 | tf_op jit(solution)/shard_map/cond/branch_1_fun/all_to_all | solution.py:223
  219.9 13.1 %branch_1_fun.13 = bf16[8,64,1024]{2,1,0:T(8,128)(2,1)S(1)} custom-call(s32[9]{0:T(128)} %get-tuple-element.126.facts_ref, bf16[8,64,1024]{2,1,0:T(8,128)(2,1)} %all_to_all.55.x_ref, bf16[4096,1024]{1,0:T(8,128)(2,1)} %get-tuple-element.127.w_out_ref, bf16[1024,4096]{1,0:T(8,128)(2,1)} %get-tuple-element.128.w_in_ref, ...), custom_call_target="tpu_custom_call" | custom-call | flops 8589934592 | bytes 16777216 | tf_op jit(solution)/shard_map/cond/branch_1_fun/pallas_call | solution.py:153
  233.0 14.0 %all_to_all.56 = bf16[8,64,1024]{2,1,0:T(8,128)(2,1)S(1)} all-to-all(bf16[8,64,1024]{2,1,0:T(8,128)(2,1)S(1)} %branch_1_fun.13), channel_id=1, replica_groups=mesh['section'=4,'replica'=4,'tensor'=8] {'tensor'}, dimensions={0} | all-to-all | bytes 2097152 | tf_op jit(solution)/shard_map/cond/branch_1_fun/all_to_all | solution.py:223
  247.1 0.2 convert_reduce_fusion.4
  247.3 0.8 shard_map.56
  248.1 13.3 %all_to_all.57 = bf16[4,8,16,1024]{3,2,1,0:T(8,128)(2,1)S(1)} all-to-all(bf16[4,8,16,1024]{3,2,1,0:T(8,128)(2,1)S(1)} %shard_map.56), channel_id=1, replica_groups=mesh['section'=4,'replica'=4,'tensor'=8] {'replica'}, dimensions={0} | all-to-all | bytes 2097152 | tf_op jit(solution)/shard_map/all_to_all | solution.py:272
  261.4 0.9 reduce_sum.84
  (18 shorter events, 0.3 us)
Async XLA Ops:
  4.3 5.5 %copy-start.4 = (s32[3,8,4]{1,2,0:T(4,128)S(1)}, s32[3,8,4]{1,2,0:T(4,128)}, u32[]{:S(2)}) copy-start(s32[3,8,4]{1,2,0:T(4,128)} %get-tuple-element.139) | copy-start | bytes 1156 | tf_op jit(solution)/shard_map/cond
  4.3 6.5 %copy-start.2 = (bf16[2,64,1024]{2,1,0:T(8,128)(2,1)S(1)}, bf16[2,64,1024]{2,1,0:T(8,128)(2,1)}, u32[]{:S(2)}) copy-start(bf16[2,64,1024]{2,1,0:T(8,128)(2,1)} %get-tuple-element.92) | copy-start | bytes 786436 | tf_op jit(solution)/shard_map/cond
  4.3 55.0 %all-to-all-start = ((bf16[4,8,128,512]{3,2,1,0:T(8,128)(2,1)}), bf16[4,8,128,512]{3,2,1,0:T(8,128)(2,1)}, u32[]{:S(2)}, u32[]{:S(2)}) async-start(bf16[4,8,128,512]{3,2,1,0:T(8,128)(2,1)} %broadcast_in_dim.37), calls=%async_computation | async-start | bytes 8388608 | tf_op jit(solution)/shard_map/cond/branch_0_fun/all_to_all | solution.py:243
  69.4 1.6 collective-permute-start
  71.1 0.7 collective-permute-start.1
  72.0 81.6 %collective-permute-start.2 = (bf16[64,1024]{1,0:T(8,128)(2,1)S(1)}, bf16[64,1024]{1,0:T(8,128)(2,1)S(1)}, u32[]{:S(2)}, u32[]{:S(2)}) collective-permute-start(bf16[64,1024]{1,0:T(8,128)(2,1)S(1)} %get-tuple-element.149.refs_2_), channel_id=1, source_target_pairs={{32,0},{64,32},{33,1},{65,33},{34,2},{66,34},{35,3},{67,35},{36,4}... | collective-permute-start | bytes 393224 | tf_op jit(solution)/shard_map/ppermute | solution.py:270
  200.9 4.4 %collective-permute-start.3 = (bf16[64,1024]{1,0:T(8,128)(2,1)S(1)}, bf16[64,1024]{1,0:T(8,128)(2,1)S(1)}, u32[]{:S(2)}, u32[]{:S(2)}) collective-permute-start(bf16[64,1024]{1,0:T(8,128)(2,1)S(1)} %get-tuple-element.150.refs_3_), channel_id=1, source_target_pairs={{32,0},{33,1},{34,2},{35,3},{36,4},{37,5},{38,6},{39,7},{40,8},{41... | collective-permute-start | bytes 393224 | tf_op jit(solution)/shard_map/ppermute | solution.py:270
where the time goes:
time: 263 us; the launch traced here: 262 us
  waiting for transfers between devices  132 us (50%)
  blocking collectives  75.8 us (29%)
  Pallas kernels  37 us (14%)
  starting transfers between devices  9.44 us (4%)
  other arithmetic  4.18 us (2%)
  local copies, waits for them, and re-layouts  3.63 us (1%)
    ppermute x4, waiting for transfers between devices, shards(): lax.ppermute(result, 'section', [(s, s - 1) for s in holders if s > 0])  83.3 us
    all_to_all x4, blocking collectives, swap(): return lax.all_to_all(value, 'tensor', 0, 0)  62.5 us
    all_to_all x1, waiting for transfers between devices, rest(): lax.all_to_all(copies, 'replica', 0, 0)  48.5 us
    pallas_call x2, Pallas kernels, block_sums(): pl.pallas_call(functools.partial(block_kernel, tuple(masks)), in_specs=[S...  26.1 us
    all_to_all x1, blocking collectives, shards(): got = lax.all_to_all(outgoing, 'replica', 0, 0)  13.3 us
    pallas_call x2, Pallas kernels, expand(): pl.pallas_call(functools.partial(expand_kernel, chunk), in_specs=[SCALARS...  10 us
    all_to_all x1, starting transfers between devices, rest(): lax.all_to_all(copies, 'replica', 0, 0)  5.52 us
  transfers between devices with their start and end apart: 5, of which 3 were waited for; matrix products, arithmetic and copies ran while one was open for 1% of the time, Pallas kernels for 0%

commit v1 on v0

--- a/solution.py
+++ b/solution.py
@@ -87,9 +87,10 @@
     )(facts, words)
 
 
-def block_kernel(holders, facts_ref, x_ref, w_out_ref, w_in_ref, *refs):
+def block_kernel(holders, fetch, facts_ref, x_ref, w_out_ref, w_in_ref, *refs):
     mask_refs, refs = refs[: len(holders)], refs[len(holders) :]
-    out_ref, w_out_buf, w_in_buf, mask_buf, hidden_ref, sems = refs
+    out_ref, w_out_buf, w_in_buf, mask_buf, hidden_ref, sems = refs[:6]
+    rows_buf = refs[6] if fetch else x_ref
     parts, rows, width = x_ref.shape
     total = parts * rows
     n_up, n_down = w_out_ref.shape[0] // BLOCK, width // COLUMNS
@@ -109,6 +110,9 @@
         columns = place(at, COLUMNS)
         return pltpu.make_async_copy(w_in_ref.at[columns], w_in_buf.at[columns], sems.at[2, at])
 
+    if fetch:
+        rows_copy = pltpu.make_async_copy(x_ref, rows_buf, refs[7])
+        rows_copy.start()
     for at in range(n_up):
         up(at).start()
         if len(holders) == 1:
@@ -122,6 +126,8 @@
 
     for at in range(n_down):
         down(at).start()
+    if fetch:
+        rows_copy.wait()
 
     @pl.loop(0, n_up)
     def _(at):
@@ -129,7 +135,7 @@
         mask(at, mask_refs[0]).wait()
         units = place(at, BLOCK)
         pre = lax.dot_general(
-            x_ref[...].reshape(total, width),
+            rows_buf[...].reshape(total, width),
             w_out_buf[units, :],
             LAST_DIMS,
             preferred_element_type=jnp.float32,
@@ -146,13 +152,13 @@
         out_ref[:, :, columns] = term.astype(jnp.bfloat16).reshape(parts, rows, COLUMNS)
 
 
-def block_sums(facts, x, w_out, w_in, masks):
+def block_sums(facts, x, w_out, w_in, masks, fetch):
     parts, rows, width = x.shape
     total = parts * rows
     units = w_out.shape[0]
     return pl.pallas_call(
-        functools.partial(block_kernel, tuple(masks)),
-        in_specs=[SCALARS, WHOLE] + [OUTSIDE] * (2 + len(masks)),
+        functools.partial(block_kernel, tuple(masks), fetch),
+        in_specs=[SCALARS, OUTSIDE if fetch else WHOLE] + [OUTSIDE] * (2 + len(masks)),
         out_specs=WHOLE,
         out_shape=jax.ShapeDtypeStruct((parts, rows, width), jnp.bfloat16),
         scratch_shapes=[
@@ -161,7 +167,8 @@
             pltpu.VMEM((parts, rows, units), jnp.bfloat16),
             pltpu.VMEM((total, units), jnp.bfloat16),
             pltpu.SemaphoreType.DMA((3, max(units // BLOCK, width // COLUMNS))),
-        ],
+        ]
+        + [pltpu.VMEM(x.shape, x.dtype), pltpu.SemaphoreType.DMA][: 2 * fetch],
         compiler_params=pltpu.CompilerParams(vmem_limit_bytes=52 * MIB),
         cost_estimate=pl.CostEstimate(
             flops=4 * total * width * units, bytes_accessed=4 * width * units, transcendentals=0
@@ -222,9 +229,9 @@
     def swap(value):
         return lax.all_to_all(value, "tensor", 0, 0)
 
-    def work(facts, rows, masks):
+    def work(facts, rows, masks, fetch=False):
         x = swap(jnp.broadcast_to(rows[None], (n_tensor,) + rows.shape))
-        partial = block_sums(facts, x, w_out_local, w_in_local, masks)
+        partial = block_sums(facts, x, w_out_local, w_in_local, masks, fetch)
         total = jnp.sum(swap(partial).astype(jnp.float32), axis=0)
         return (rows.astype(jnp.float32) + total).astype(jnp.bfloat16)
 
@@ -234,7 +241,7 @@
     def start(entry, relu_mask, route):
         facts = jnp.where(jnp.arange(1 + micro) == 0, section, replica).astype(jnp.int32)
         masks = expand_all(facts, relu_mask[0].astype(jnp.bfloat16))
-        return [work(facts, entry[0], {last: masks[0]}), facts] + masks
+        return [work(facts, entry[0], {last: masks[0]}, True), facts] + masks
 
     def rest(entry, relu_mask, route):
         words = relu_mask[0, 0].astype(jnp.bfloat16)

time: 263 us -> 266 us (1.011)
  blocking collectives: 75.8 us -> 78.5 us
    all_to_all x1, blocking collectives: 13.3 us -> 16 us  [shards(): got = lax.all_to_all(outgoing, 'replica', 0, 0)]
where the time goes in v1:
time: 266 us; the launch traced here: 265 us
  waiting for transfers between devices  132 us (50%)
  blocking collectives  78.5 us (30%)
  Pallas kernels  37 us (14%)
  starting transfers between devices  9.44 us (4%)
  other arithmetic  4.18 us (2%)
  local copies, waits for them, and re-layouts  3.63 us (1%)
    ppermute x4, waiting for transfers between devices, shards(): lax.ppermute(result, 'section', [(s, s - 1) for s in holders if s > 0])  83.3 us
    all_to_all x4, blocking collectives, swap(): return lax.all_to_all(value, 'tensor', 0, 0)  62.5 us
    all_to_all x1, waiting for transfers between devices, rest(): lax.all_to_all(copies, 'replica', 0, 0)  48.5 us
    pallas_call x2, Pallas kernels, block_sums(): pl.pallas_call(functools.partial(block_kernel, tuple(masks), fetch), in_s...  26.1 us
    all_to_all x1, blocking collectives, shards(): got = lax.all_to_all(outgoing, 'replica', 0, 0)  16 us
    pallas_call x2, Pallas kernels, expand(): pl.pallas_call(functools.partial(expand_kernel, chunk), in_specs=[SCALARS...  10 us
    all_to_all x1, starting transfers between devices, rest(): lax.all_to_all(copies, 'replica', 0, 0)  5.52 us
  transfers between devices with their start and end apart: 5, of which 3 were waited for; matrix products, arithmetic and copies ran while one was open for 1% of the time, Pallas kernels for 0%

profile of v1, /device:TPU:0, one launch (start us, length us, event | category | flops | bytes accessed | tf_op | source)
XLA Modules:
  0.0 265.1 jit_solution(4551914813631724491)
XLA Ops:
  0.0 69.4 %conditional.5 = (bf16[64,1024]{1,0:T(8,128)(2,1)S(1)}, s32[9]{0:T(128)}, bf16[8,64,4096]{2,1,0:T(8,128)(2,1)}, bf16[8,64,4096]{2,1,0:T(8,128)(2,1)}) conditional(s32[]{:T(128)} %convert_element_type.77, (bf16[2,64,1024]{2,1,0:T(8,128)(2,1)}, s32[]{:T(128)}, s32[]{:T(128)}, s32[4]{0:T(128)S(1)}, s32[3,8,4]{1,2,0:T(4,128)}, /*index=5*/s32[4]{0:T(128)S(1)}, ...), branch_computations={%region_0.4_spmd, %region_4.6_spmd} | conditional | flops 10739122176 | bytes 52560096 | solution.py:261
  0.0 1.9 convert_bitcast_fusion
  1.9 2.5 broadcast_in_dim.37
  4.3 5.5 %all-to-all-start = ((bf16[4,8,128,512]{3,2,1,0:T(8,128)(2,1)}), bf16[4,8,128,512]{3,2,1,0:T(8,128)(2,1)}, u32[]{:S(2)}, u32[]{:S(2)}) async-start(bf16[4,8,128,512]{3,2,1,0:T(8,128)(2,1)} %broadcast_in_dim.37), calls=%async_computation | async-start | bytes 8388608 | tf_op jit(solution)/shard_map/cond/branch_0_fun/all_to_all | solution.py:250
  10.1 0.1 fusion
  10.2 0.7 pad_add_fusion.facts_ref
  10.8 48.5 %all-to-all-done.words_ref = bf16[4,8,128,512]{3,2,1,0:T(8,128)(2,1)} async-done(((bf16[4,8,128,512]{3,2,1,0:T(8,128)(2,1)}), bf16[4,8,128,512]{3,2,1,0:T(8,128)(2,1)}, u32[]{:S(2)}, u32[]{:S(2)}) %all-to-all-start) | async-done | bytes 4194336 | tf_op jit(solution)/shard_map/cond/branch_0_fun/all_to_all | solution.py:250
  59.3 5.0 %branch_0_fun.2 = bf16[8,64,4096]{2,1,0:T(8,128)(2,1)} custom-call(s32[9]{0:T(128)} %pad_add_fusion.facts_ref, bf16[4,8,128,512]{3,2,1,0:T(8,128)(2,1)} %all-to-all-done.words_ref), custom_call_target="tpu_custom_call" | custom-call | flops 1073741824 | bytes 4718592 | tf_op jit(solution)/shard_map/cond/branch_0_fun/pallas_call | solution.py:70
  64.4 5.0 %branch_0_fun.3 = bf16[8,64,4096]{2,1,0:T(8,128)(2,1)} custom-call(s32[9]{0:T(128)} %pad_add_fusion.facts_ref, bf16[4,8,128,512]{3,2,1,0:T(8,128)(2,1)} %all-to-all-done.words_ref), custom_call_target="tpu_custom_call" | custom-call | flops 1073741824 | bytes 4718592 | tf_op jit(solution)/shard_map/cond/branch_0_fun/pallas_call | solution.py:70
  69.4 0.7 collective-permute-start
  70.1 0.9 slice.19
  71.1 0.7 collective-permute-start.1
  71.8 0.2 conditional.7
  72.0 1.3 collective-permute-start.2
  73.3 80.3 %collective-permute-done.2 = bf16[64,1024]{1,0:T(8,128)(2,1)S(1)} collective-permute-done((bf16[64,1024]{1,0:T(8,128)(2,1)S(1)}, bf16[64,1024]{1,0:T(8,128)(2,1)S(1)}, u32[]{:S(2)}, u32[]{:S(2)}) %collective-permute-start.2) | collective-permute-done | bytes 131104 | tf_op jit(solution)/shard_map/ppermute | solution.py:277
  153.6 47.3 %conditional.8 = (bf16[64,1024]{1,0:T(8,128)(2,1)S(1)}) conditional(s32[]{:T(128)} %convert_element_type.80, bf16[64,1024]{1,0:T(8,128)(2,1)S(1)} %collective-permute-done.2, (bf16[64,1024]{1,0:T(8,128)(2,1)S(1)}, s32[9]{0:T(128)}, bf16[4096,1024]{1,0:T(8,128)(2,1)}, bf16[1024,4096]{1,0:T(8,128)(2,1)}, bf16[8,64,4096]{2,1,0:T(8,128)(2,1)}, ...), branch_computations={%region_12.13_spmd, %region_13.15_spmd} | conditional | flops 8591114240 | bytes 23986184 | solution.py:266
  153.6 0.1 broadcast_in_dim.51
  153.7 16.1 %all_to_all.53.x_ref = bf16[8,64,1024]{2,1,0:T(8,128)(2,1)} all-to-all(bf16[8,64,1024]{2,1,0:T(8,128)(2,1)S(1)} %broadcast_in_dim.51), channel_id=1, replica_groups=mesh['section'=4,'replica'=4,'tensor'=8] {'tensor'}, dimensions={0} | all-to-all | bytes 2097152 | tf_op jit(solution)/shard_map/cond/branch_1_fun/all_to_all | solution.py:230
  169.8 13.1 %branch_1_fun.12 = bf16[8,64,1024]{2,1,0:T(8,128)(2,1)S(1)} custom-call(s32[9]{0:T(128)} %get-tuple-element.120.facts_ref, bf16[8,64,1024]{2,1,0:T(8,128)(2,1)} %all_to_all.53.x_ref, bf16[4096,1024]{1,0:T(8,128)(2,1)} %get-tuple-element.121.w_out_ref, bf16[1024,4096]{1,0:T(8,128)(2,1)} %get-tuple-element.122.w_in_ref, ...), custom_call_target="tpu_custom_call" | custom-call | flops 8589934592 | bytes 16777216 | tf_op jit(solution)/shard_map/cond/branch_1_fun/pallas_call | solution.py:159
  182.9 17.8 %all_to_all.54 = bf16[8,64,1024]{2,1,0:T(8,128)(2,1)S(1)} all-to-all(bf16[8,64,1024]{2,1,0:T(8,128)(2,1)S(1)} %branch_1_fun.12), channel_id=1, replica_groups=mesh['section'=4,'replica'=4,'tensor'=8] {'tensor'}, dimensions={0} | all-to-all | bytes 2097152 | tf_op jit(solution)/shard_map/cond/branch_1_fun/all_to_all | solution.py:230
  200.7 0.2 convert_reduce_fusion.3
  200.9 1.3 collective-permute-start.3
  202.2 3.0 %collective-permute-done.3 = bf16[64,1024]{1,0:T(8,128)(2,1)S(1)} collective-permute-done((bf16[64,1024]{1,0:T(8,128)(2,1)S(1)}, bf16[64,1024]{1,0:T(8,128)(2,1)S(1)}, u32[]{:S(2)}, u32[]{:S(2)}) %collective-permute-start.3) | collective-permute-done | bytes 131104 | tf_op jit(solution)/shard_map/ppermute | solution.py:277
  205.2 42.0 %conditional.9 = (bf16[64,1024]{1,0:T(8,128)(2,1)S(1)}) conditional(s32[]{:T(128)} %convert_element_type.81, bf16[64,1024]{1,0:T(8,128)(2,1)S(1)} %collective-permute-done.3, (bf16[64,1024]{1,0:T(8,128)(2,1)S(1)}, s32[9]{0:T(128)}, bf16[4096,1024]{1,0:T(8,128)(2,1)}, bf16[1024,4096]{1,0:T(8,128)(2,1)}, bf16[8,64,4096]{2,1,0:T(8,128)(2,1)}) %tuple.64), branch_computations={%region_15.16_spmd, %region_16.18_spmd} | conditional | flops 8591114240 | bytes 23986184 | solution.py:266
  205.2 0.1 broadcast_in_dim.52
  205.3 14.6 %all_to_all.55.x_ref = bf16[8,64,1024]{2,1,0:T(8,128)(2,1)} all-to-all(bf16[8,64,1024]{2,1,0:T(8,128)(2,1)S(1)} %broadcast_in_dim.52), channel_id=1, replica_groups=mesh['section'=4,'replica'=4,'tensor'=8] {'tensor'}, dimensions={0} | all-to-all | bytes 2097152 | tf_op jit(solution)/shard_map/cond/branch_1_fun/all_to_all | solution.py:230
  219.9 13.1 %branch_1_fun.13 = bf16[8,64,1024]{2,1,0:T(8,128)(2,1)S(1)} custom-call(s32[9]{0:T(128)} %get-tuple-element.126.facts_ref, bf16[8,64,1024]{2,1,0:T(8,128)(2,1)} %all_to_all.55.x_ref, bf16[4096,1024]{1,0:T(8,128)(2,1)} %get-tuple-element.127.w_out_ref, bf16[1024,4096]{1,0:T(8,128)(2,1)} %get-tuple-element.128.w_in_ref, ...), custom_call_target="tpu_custom_call" | custom-call | flops 8589934592 | bytes 16777216 | tf_op jit(solution)/shard_map/cond/branch_1_fun/pallas_call | solution.py:159
  233.0 14.0 %all_to_all.56 = bf16[8,64,1024]{2,1,0:T(8,128)(2,1)S(1)} all-to-all(bf16[8,64,1024]{2,1,0:T(8,128)(2,1)S(1)} %branch_1_fun.13), channel_id=1, replica_groups=mesh['section'=4,'replica'=4,'tensor'=8] {'tensor'}, dimensions={0} | all-to-all | bytes 2097152 | tf_op jit(solution)/shard_map/cond/branch_1_fun/all_to_all | solution.py:230
  247.1 0.2 convert_reduce_fusion.4
  247.3 0.8 shard_map.56
  248.1 16.0 %all_to_all.57 = bf16[4,8,16,1024]{3,2,1,0:T(8,128)(2,1)S(1)} all-to-all(bf16[4,8,16,1024]{3,2,1,0:T(8,128)(2,1)S(1)} %shard_map.56), channel_id=1, replica_groups=mesh['section'=4,'replica'=4,'tensor'=8] {'replica'}, dimensions={0} | all-to-all | bytes 2097152 | tf_op jit(solution)/shard_map/all_to_all | solution.py:279
  264.1 0.9 reduce_sum.84
  (18 shorter events, 0.3 us)
Async XLA Ops:
  4.3 5.5 %copy-start.4 = (s32[3,8,4]{1,2,0:T(4,128)S(1)}, s32[3,8,4]{1,2,0:T(4,128)}, u32[]{:S(2)}) copy-start(s32[3,8,4]{1,2,0:T(4,128)} %get-tuple-element.139) | copy-start | bytes 1156 | tf_op jit(solution)/shard_map/cond
  4.3 6.5 %copy-start.2 = (bf16[2,64,1024]{2,1,0:T(8,128)(2,1)S(1)}, bf16[2,64,1024]{2,1,0:T(8,128)(2,1)}, u32[]{:S(2)}) copy-start(bf16[2,64,1024]{2,1,0:T(8,128)(2,1)} %get-tuple-element.92) | copy-start | bytes 786436 | tf_op jit(solution)/shard_map/cond
  4.3 55.0 %all-to-all-start = ((bf16[4,8,128,512]{3,2,1,0:T(8,128)(2,1)}), bf16[4,8,128,512]{3,2,1,0:T(8,128)(2,1)}, u32[]{:S(2)}, u32[]{:S(2)}) async-start(bf16[4,8,128,512]{3,2,1,0:T(8,128)(2,1)} %broadcast_in_dim.37), calls=%async_computation | async-start | bytes 8388608 | tf_op jit(solution)/shard_map/cond/branch_0_fun/all_to_all | solution.py:250
  69.4 1.6 collective-permute-start
  71.1 0.7 collective-permute-start.1
  72.0 81.6 %collective-permute-start.2 = (bf16[64,1024]{1,0:T(8,128)(2,1)S(1)}, bf16[64,1024]{1,0:T(8,128)(2,1)S(1)}, u32[]{:S(2)}, u32[]{:S(2)}) collective-permute-start(bf16[64,1024]{1,0:T(8,128)(2,1)S(1)} %get-tuple-element.149.refs_2_), channel_id=1, source_target_pairs={{32,0},{64,32},{33,1},{65,33},{34,2},{66,34},{35,3},{67,35},{36,4}... | collective-permute-start | bytes 393224 | tf_op jit(solution)/shard_map/ppermute | solution.py:277
  200.9 4.4 %collective-permute-start.3 = (bf16[64,1024]{1,0:T(8,128)(2,1)S(1)}, bf16[64,1024]{1,0:T(8,128)(2,1)S(1)}, u32[]{:S(2)}, u32[]{:S(2)}) collective-permute-start(bf16[64,1024]{1,0:T(8,128)(2,1)S(1)} %get-tuple-element.150.refs_3_), channel_id=1, source_target_pairs={{32,0},{33,1},{34,2},{35,3},{36,4},{37,5},{38,6},{39,7},{40,8},{41... | collective-permute-start | bytes 393224 | tf_op jit(solution)/shard_map/ppermute | solution.py:277
